TPU v7x, 32 devices: a whole 2x2x4 slice. The times are simulated.
32 devices in a mesh: row: 4 (over z), col: 4 (over y, x), dep: 2 (over core).
Axes of the slice: x: 2, y: 2, z: 4, core: 2. Of those that a mesh axis runs over, the one named last changes fastest.
Arguments:
- load: float32 [3, 8, 32, 32, 1024], P(None, None, 'row', 'col', 'dep'), may hold values from -6 to 6
- diagonal_block: float32 [3, 3, 32, 32, 1024], P(None, None, 'row', 'col', 'dep'), may hold values from -0.3 to 12, as said below
- coupling: float32 [6, 3, 3, 32, 32, 1024], P(None, None, None, 'row', 'col', 'dep'), may hold values from -0.15 to 0.15
- aggregates: int32 [32, 32, 1024], P('row', 'col', 'dep'), may hold values from 0 to 63, as said below
- coarse_inverse: float32 [4, 2, 768, 768], P('col', 'dep'), may hold values from -0.02 to 0.03
Outputs:
- correction: float32 [3, 8, 32, 32, 1024], P(None, None, 'row', 'col', 'dep')
Inputs may be any that keep to these rules, and one draw needn't show every extreme that they name: Each device's nodes form 64 nonempty aggregates of nearby nodes, numbered locally. `diagonal_block`: diagonally dominant blocks with positive diagonal.
All inputs are finite; a program needn't handle non-finite values.
Results may differ from a plain program's by a relative error of at most 0.00005.
Values sent between devices are 32-bit elements; how exact they have to be, the bound alone decides.
A program may use at most 128 MiB of HBM per device.

v0:
```python
import functools

import jax
import jax.numpy as jnp
from jax import lax
from jax.experimental import pallas as pl
from jax.experimental.pallas import tpu as pltpu
from jax.sharding import PartitionSpec as P

LANES = 128
SUB = 8
MESH = pl.DeviceIdType.MESH


def kernel(
    n_row, n_col, agg,
    load_h, diag_h, coup_h, aggr_h, inv_h, out_h,
    load_v, diag_v, coup, ag, inv, wgt, first, second, resid, third, out_v,
    xh, yh, ys, agx, agy, agys, agz, gath, tabs,
    in_sem, send_sem, recv_sem, g_send, g_recv, out_sem,
):
    rhs, xs = load_v.shape[1], load_v.shape[2]
    zts = load_v.shape[4] // LANES
    rows = 3 * rhs * SUB
    rb = 4
    row, col, dep = lax.axis_index("row"), lax.axis_index("col"), lax.axis_index("dep")
    other = 1 - dep
    own_rows = 3 * agg

    copies = [
        pltpu.make_async_copy(diag_h, diag_v, in_sem.at[0]),
        pltpu.make_async_copy(load_h, load_v, in_sem.at[1]),
        pltpu.make_async_copy(aggr_h, ag, in_sem.at[2]),
        pltpu.make_async_copy(coup_h, coup, in_sem.at[3]),
        pltpu.make_async_copy(
            inv_h.at[0, 0, pl.ds(pl.multiple_of(row * own_rows, SUB), own_rows), :], inv, in_sem.at[4]
        ),
    ]
    for copy in copies:
        copy.start()

    sides = [
        (row > 0, {"row": row - 1}),
        (row < n_row - 1, {"row": row + 1}),
        (col > 0, {"col": col - 1}),
        (col < n_col - 1, {"col": col + 1}),
    ]
    barrier = pltpu.get_barrier_semaphore()
    for step in range(1, n_row):
        pl.semaphore_signal(barrier, inc=1, device_id={"row": lax.rem(row + step, n_row)}, device_id_type=MESH)
    for has, device in sides[2:]:
        @pl.when(has)
        def _():
            pl.semaphore_signal(barrier, inc=1, device_id=device, device_id_type=MESH)
    pl.semaphore_signal(barrier, inc=1, device_id={"dep": other}, device_id_type=MESH)

    def zlane(zt):
        return pl.ds(pl.multiple_of(zt * LANES, LANES), LANES)

    def zero_edges(field):
        def body(zt, _):
            field[0, zt + 1] = jnp.zeros((rows, LANES), jnp.float32)
            field[xs + 1, zt + 1] = jnp.zeros((rows, LANES), jnp.float32)
            return 0

        lax.fori_loop(0, zts, body, 0)
        side = dep * (zts + 1)

        def body_z(x, _):
            field[x + 1, side] = jnp.zeros((rows, LANES), jnp.float32)
            return 0

        lax.fori_loop(0, xs, body_z, 0)

    zero_edges(first)
    copies[0].wait()
    copies[1].wait()

    def scale(x, _):
        for c in range(3):
            wgt[c, x] = 0.8 / diag_v[c, c, x]

        def inner(zt, _):
            for c in range(3):
                value = wgt[c, x, :, zlane(zt)][None] * load_v[c, :, x, :, zlane(zt)]
                first[x + 1, zt + 1, c * rhs * SUB:(c + 1) * rhs * SUB, :] = value.reshape(rhs * SUB, LANES)
            return 0

        lax.fori_loop(0, zts, inner, 0)
        return 0

    lax.fori_loop(0, xs, scale, 0)

    def pack_y(field, slot):
        def body(i, _):
            x, zt = i // zts, i % zts
            for s in range(2):
                ys[slot, s, x, zt] = field[x + 1, zt + 1, pl.ds(s * (SUB - 1), 3 * rhs, stride=SUB), :]
            return 0

        lax.fori_loop(0, xs * zts, body, 0)

    def remote(src, dst, sem, device):
        return pltpu.make_async_remote_copy(
            src_ref=src, dst_ref=dst, send_sem=send_sem.at[sem], recv_sem=recv_sem.at[sem],
            device_id=device, device_id_type=MESH,
        )

    def to_sides(base, pieces):
        found = []
        for s, (has, device) in enumerate(sides):
            src, dst = pieces[s]
            found.append((has, remote(src, dst, base + (s ^ 1), device)))
        return found

    def from_sides(base, pieces):
        found = []
        for s, (has, device) in enumerate(sides):
            src, dst = pieces[s ^ 1]
            found.append((has, remote(src, dst, base + s, device)))
        return found

    def start_all(found, only=range(4)):
        for s in only:
            has, copy = found[s]
            pl.when(has)(copy.start)

    def wait_sends(found):
        for has, copy in found:
            pl.when(has)(copy.wait_send)

    def face_pieces(field, slot):
        return [
            (field.at[1, pl.ds(1, zts)], xh.at[slot, 1]),
            (field.at[xs, pl.ds(1, zts)], xh.at[slot, 0]),
            (ys.at[slot, 0], yh.at[slot, 1]),
            (ys.at[slot, 1], yh.at[slot, 0]),
        ]

    own_z = (1 - dep) * (zts - 1) + 1
    halo_z = (1 - dep) * (zts + 1)
    far_z = dep * (zts + 1)

    def z_copy(field, sem):
        return remote(field.at[pl.ds(1, xs), own_z], field.at[pl.ds(1, xs), far_z], sem, {"dep": other})

    pack_y(first, 0)
    pl.semaphore_wait(barrier, n_row - 1 + 1 + (col > 0).astype(jnp.int32) + (col < n_col - 1).astype(jnp.int32))
    p1 = face_pieces(first, 0)
    e1 = to_sides(0, p1)
    start_all(e1, (2, 3, 0, 1))
    z1 = z_copy(first, 4)
    z1.start()

    copies[2].wait()
    for x in range(xs):
        for s in range(2):
            y = s * (SUB - 1)
            agys[s, x:x + 1, :] = ag[x, y:y + 1, :]
    pa = [
        (ag.at[0], agx.at[1]), (ag.at[xs - 1], agx.at[0]),
        (agys.at[0], agy.at[1]), (agys.at[1], agy.at[0]),
    ]
    ea = to_sides(10, pa)
    start_all(ea)
    za = remote(
        ag.at[:, :, zlane((1 - dep) * (zts - 1))], agz, 14, {"dep": other}
    )
    za.start()
    zero_edges(second)
    zero_edges(third)
    tabs[...] = jnp.zeros_like(tabs)
    gath[row] = jnp.zeros((3 * rhs, LANES), jnp.float32)
    copies[3].wait()
    z1.wait_recv()

    lane = lax.broadcasted_iota(jnp.int32, (rb, SUB, LANES), 2)
    sub = lax.broadcasted_iota(jnp.int32, (rb, SUB, LANES), 1)
    at_first, at_last = lane == 0, lane == LANES - 1
    at_top, at_bottom = sub == 0, sub == SUB - 1

    def tile_rows(c, r0):
        return slice((c * rhs + r0) * SUB, (c * rhs + r0 + rb) * SUB)

    def tile(field, x, zt, c, r0):
        return field[x, zt, tile_rows(c, r0), :].reshape(rb, SUB, LANES)

    def operate(field, x, zt, r0):
        own = [tile(field, x + 1, zt + 1, c, r0) for c in range(3)]
        zl = zlane(zt)
        total = []
        for a in range(3):
            t = diag_v[a, 0, x, :, zl][None] * own[0]
            for c in (1, 2):
                t = t + diag_v[a, c, x, :, zl][None] * own[c]
            total.append(t)
        for d in range(6):
            for c in range(3):
                if d == 0:
                    near = tile(field, x + 2, zt + 1, c, r0)
                elif d == 1:
                    near = tile(field, x, zt + 1, c, r0)
                elif d == 2:
                    near = jnp.where(at_bottom, 0.0, pltpu.roll(own[c], SUB - 1, 1))
                elif d == 3:
                    near = jnp.where(at_top, 0.0, pltpu.roll(own[c], 1, 1))
                elif d == 4:
                    near = pltpu.roll(jnp.where(at_first, tile(field, x + 1, zt + 2, c, r0), own[c]), LANES - 1, 2)
                else:
                    near = pltpu.roll(jnp.where(at_last, tile(field, x + 1, zt, c, r0), own[c]), 1, 2)
                for a in range(3):
                    total[a] = total[a] - coup[d, a, c, x, :, zl][None] * near
        return own, total

    def sweep(body):
        def run(i, _):
            x, zt = i // zts, i % zts
            for r0 in range(0, rhs, rb):
                body(x, zt, r0)
            return 0

        lax.fori_loop(0, xs * zts, run, 0)

    def smooth(x, zt, r0):
        own, total = operate(first, x, zt, r0)
        zl = zlane(zt)
        for a in range(3):
            value = own[a] + wgt[a, x, :, zl][None] * (load_v[a, r0:r0 + rb, x, :, zl] - total[a])
            second[x + 1, zt + 1, tile_rows(a, r0), :] = value.reshape(rb * SUB, LANES)

    sweep(smooth)

    def fix_x(field, off, s, slot, weighted):
        x = s * (xs - 1)
        d = 1 - s

        def body(zt, _):
            zl = zlane(zt)
            for r0 in range(0, rhs, rb):
                near = [xh[slot, s, zt, tile_rows(c, r0), :].reshape(rb, SUB, LANES) for c in range(3)]
                for a in range(3):
                    t = coup[d, a, 0, x, :, zl][None] * near[0]
                    for c in (1, 2):
                        t = t + coup[d, a, c, x, :, zl][None] * near[c]
                    t = t.reshape(rb * SUB, LANES)
                    if weighted:
                        t = (wgt[a, x, :, zl][None] * t.reshape(rb, SUB, LANES)).reshape(rb * SUB, LANES)
                        field[x + off, zt + off, tile_rows(a, r0), :] += t
                    else:
                        field[x + off, zt + off, tile_rows(a, r0), :] += t
            return 0

        lax.fori_loop(0, zts, body, 0)

    def fix_y(field, off, s, slot, weighted):
        y = s * (SUB - 1)
        d = 3 - s

        def body(i, _):
            x, zt = i // zts, i % zts
            zl = zlane(zt)
            near = [yh[slot, s, x, zt, c * rhs:(c + 1) * rhs, :] for c in range(3)]
            for a in range(3):
                t = coup[d, a, 0, x, y:y + 1, zl] * near[0]
                for c in (1, 2):
                    t = t + coup[d, a, c, x, y:y + 1, zl] * near[c]
                if weighted:
                    t = wgt[a, x, y:y + 1, zl] * t
                at = pl.ds(a * rhs * SUB + y, rhs, stride=SUB)
                field[x + off, zt + off, at, :] = field[x + off, zt + off, at, :] + t
            return 0

        lax.fori_loop(0, xs * zts, body, 0)

    def fix_arrived(arrivals, field, off, slot, weighted):
        for s, (has, copy) in enumerate(arrivals):
            @pl.when(has)
            def _():
                if copy is not None:
                    copy.wait_recv()
                if s < 2:
                    fix_x(field, off, s, slot, weighted)
                else:
                    fix_y(field, off, s - 2, slot, weighted)

    fix_arrived(from_sides(0, p1), second, 1, 0, True)
    pack_y(second, 1)
    p2 = face_pieces(second, 1)
    e2 = to_sides(5, p2)
    start_all(e2, (2, 3, 0, 1))
    z2 = z_copy(second, 9)
    z2.start()
    z2.wait_recv()

    def defect(x, zt, r0):
        own, total = operate(second, x, zt, r0)
        zl = zlane(zt)
        for a in range(3):
            value = load_v[a, r0:r0 + rb, x, :, zl] - total[a]
            resid[x, zt, tile_rows(a, r0), :] = value.reshape(rb * SUB, LANES)

    sweep(defect)
    copies[4].wait()
    fix_arrived(from_sides(5, p2), resid, 0, 1, False)

    number = lax.broadcasted_iota(jnp.int32, (agg, zts * LANES), 0)

    def restrict(x, total):
        for y in range(SUB):
            value = jnp.concatenate(
                [resid[x, zt, pl.ds(y, 3 * rhs, stride=SUB), :] for zt in range(zts)], axis=1
            )
            high = value.astype(jnp.bfloat16).astype(jnp.float32)
            both = jnp.concatenate([high, value - high], axis=0).astype(jnp.bfloat16)
            member = (ag[x, y:y + 1, :] == number).astype(jnp.float32).astype(jnp.bfloat16)
            total = total + lax.dot_general(
                both, member, (((1,), (1,)), ((), ())), preferred_element_type=jnp.float32
            )
        return total

    sums = lax.fori_loop(0, xs, restrict, jnp.zeros((6 * rhs, agg), jnp.float32))
    gath[row, :, 0:agg] = sums[:3 * rhs] + sums[3 * rhs:]
    gathers = []
    for step in range(1, n_row):
        copy = pltpu.make_async_remote_copy(
            src_ref=gath.at[row], dst_ref=gath.at[row], send_sem=g_send.at[step - 1], recv_sem=g_recv.at[step - 1],
            device_id={"row": lax.rem(row + step, n_row)}, device_id_type=MESH,
        )
        copy.start()
        gathers.append(copy)
    for step in range(1, n_row):
        source = lax.rem(row + n_row - step, n_row)
        pltpu.make_async_remote_copy(
            src_ref=gath.at[source], dst_ref=gath.at[source], send_sem=g_send.at[step - 1],
            recv_sem=g_recv.at[step - 1], device_id={"row": source}, device_id_type=MESH,
        ).wait_recv()
    vector = jnp.concatenate(
        [gath[i, c * rhs:(c + 1) * rhs, 0:agg] for i in range(n_row) for c in range(3)], axis=1
    )
    solved = lax.dot_general(
        vector, inv[...], (((1,), (1,)), ((), ())), precision=lax.Precision.HIGHEST,
        preferred_element_type=jnp.float32,
    )
    for c in range(3):
        tabs[0, c * rhs:(c + 1) * rhs, 0:agg] = solved[:, c * agg:(c + 1) * agg]
    pt = [(tabs.at[0], tabs.at[1 + (s ^ 1)]) for s in range(4)]
    et = to_sides(15, pt)
    start_all(et)
    zt_copy = remote(tabs.at[0], tabs.at[5], 19, {"dep": other})
    zt_copy.start()

    def look(table, index):
        return jnp.take_along_axis(table, index, axis=1, mode="promise_in_bounds")

    def spread(i, _):
        x, zt = i // zts, i % zts
        index = ag[x, :, zlane(zt)]
        for k in range(3 * rhs):
            table = jnp.broadcast_to(tabs[0, k:k + 1, :], (SUB, LANES))
            third[x + 1, zt + 1, k * SUB:(k + 1) * SUB, :] = look(table, index)
        return 0

    lax.fori_loop(0, xs * zts, spread, 0)
    zt_copy.wait_recv()
    za.wait_recv()

    def spread_z(x, _):
        index = agz[x]
        for k in range(3 * rhs):
            table = jnp.broadcast_to(tabs[5, k:k + 1, :], (SUB, LANES))
            third[x + 1, halo_z, k * SUB:(k + 1) * SUB, :] = look(table, index)
        return 0

    lax.fori_loop(0, xs, spread_z, 0)

    def final(x, zt, r0):
        own, total = operate(third, x, zt, r0)
        zl = zlane(zt)
        for a in range(3):
            left = resid[x, zt, tile_rows(a, r0), :].reshape(rb, SUB, LANES) - total[a]
            value = tile(second, x + 1, zt + 1, a, r0) + own[a] + wgt[a, x, :, zl][None] * left
            out_v[x, zt, tile_rows(a, r0), :] = value.reshape(rb * SUB, LANES)

    sweep(final)

    arrived_t, arrived_a = from_sides(15, pt), from_sides(10, pa)
    for s in range(4):
        has = sides[s][0]

        @pl.when(has)
        def _():
            arrived_t[s][1].wait_recv()
            arrived_a[s][1].wait_recv()
            if s < 2:
                def body(zt, _):
                    index = agx[s, :, zlane(zt)]
                    for k in range(3 * rhs):
                        table = jnp.broadcast_to(tabs[1 + s, k:k + 1, :], (SUB, LANES))
                        xh[2, s, zt, k * SUB:(k + 1) * SUB, :] = look(table, index)
                    return 0

                lax.fori_loop(0, zts, body, 0)
                fix_x(out_v, 0, s, 2, True)
            else:
                def body(zt, _):
                    for x in range(xs):
                        index = jnp.broadcast_to(agy[s - 2, x:x + 1, zlane(zt)], (SUB, LANES))
                        for c in range(3):
                            yh[2, s - 2, x, zt, c * rhs:(c + 1) * rhs, :] = look(
                                tabs[1 + s, c * rhs:(c + 1) * rhs, :], index
                            )
                    return 0

                lax.fori_loop(0, zts, body, 0)
                fix_y(out_v, 0, s - 2, 2, True)

    outs = []
    for x in range(xs):
        for zt in range(zts):
            outs.append(pltpu.make_async_copy(
                out_v.at[x, zt].reshape(3, rhs, SUB, LANES),
                out_h.at[:, :, x, :, pl.ds(zt * LANES, LANES)],
                out_sem.at[x * zts + zt],
            ))
    for copy in outs:
        copy.start()
    for found in (e1, e2, ea, et):
        wait_sends(found)
    for copy in (z1, z2, za, zt_copy, *gathers):
        copy.wait_send()
    for copy in outs:
        copy.wait()


def on_device(n_row, n_col, load, diagonal_block, coupling, aggregates, coarse_inverse):
    _, rhs, xs, sub, depth = load.shape
    zts = depth // LANES
    ncg = coarse_inverse.shape[-1]
    agg = ncg // n_row // 3
    rows = 3 * rhs * sub
    f32 = jnp.float32
    dma = pltpu.SemaphoreType.DMA
    field = pltpu.VMEM((xs + 2, zts + 2, rows, LANES), f32)
    block = pltpu.VMEM((xs, zts, rows, LANES), f32)
    return pl.pallas_call(
        functools.partial(kernel, n_row, n_col, agg),
        out_shape=jax.ShapeDtypeStruct(load.shape, f32),
        in_specs=[pl.BlockSpec(memory_space=pl.ANY)] * 5,
        out_specs=pl.BlockSpec(memory_space=pl.ANY),
        scratch_shapes=[
            pltpu.VMEM(load.shape, f32),
            pltpu.VMEM(diagonal_block.shape, f32),
            pltpu.VMEM(coupling.shape, f32),
            pltpu.VMEM(aggregates.shape, jnp.int32),
            pltpu.VMEM((3 * agg, ncg), f32),
            pltpu.VMEM((3, xs, sub, depth), f32),
            field, field, block, field, block,
            pltpu.VMEM((3, 2, zts, rows, LANES), f32),
            pltpu.VMEM((3, 2, xs, zts, 3 * rhs, LANES), f32),
            pltpu.VMEM((2, 2, xs, zts, 3 * rhs, LANES), f32),
            pltpu.VMEM((2, sub, depth), jnp.int32),
            pltpu.VMEM((2, xs, depth), jnp.int32),
            pltpu.VMEM((2, xs, depth), jnp.int32),
            pltpu.VMEM((xs, sub, LANES), jnp.int32),
            pltpu.VMEM((n_row, 3 * rhs, LANES), f32),
            pltpu.VMEM((6, 3 * rhs, LANES), f32),
            dma((5,)),
            dma((20,)),
            dma((20,)),
            dma((n_row - 1,)),
            dma((n_row - 1,)),
            dma((xs * zts,)),
        ],
        compiler_params=pltpu.CompilerParams(
            collective_id=0, has_side_effects=True, vmem_limit_bytes=60 * 2**20
        ),
    )(load, diagonal_block, coupling, aggregates, coarse_inverse)


def solution(mesh):
    in_specs = (
        P(None, None, "row", "col", "dep"),
        P(None, None, "row", "col", "dep"),
        P(None, None, None, "row", "col", "dep"),
        P("row", "col", "dep"),
        P("col", "dep", None, None),
    )
    out_specs = P(None, None, "row", "col", "dep")
    return jax.shard_map(
        functools.partial(on_device, mesh.shape["row"], mesh.shape["col"]),
        mesh=mesh, in_specs=in_specs, out_specs=out_specs, check_vma=False,
    )
```

profile of v0, /device:TPU:4, one launch (start us, length us, event | category | flops | bytes accessed | tf_op | source)
XLA Modules:
  0.0 69.7 jit_solution(11769183834446167224)
XLA Ops:
  0.0 65.7 %shard_map.55 = f32[3,8,8,8,512]{4,3,2,1,0:T(8,128)} custom-call(f32[3,8,8,8,512]{4,3,2,1,0:T(8,128)} %load_h.1, f32[3,3,8,8,512]{4,3,2,1,0:T(8,128)} %diag_h.1, f32[6,3,3,8,8,512]{5,4,3,2,1,0:T(8,128)} %coup_h.1, s32[8,8,512]{2,1,0:T(8,128)} %aggr_h.1, f32[1,1,768,768]{3,2,1,0:T(8,128)} %inv_h.1), custom_call_target="tpu_custom_call" | custom-call | tf_op jit(solution)/shard_map/pallas_call | solution.py:445
  65.7 4.0 %copy.7 = f32[3,8,8,8,512]{4,3,2,1,0:T(8,128)} copy(f32[3,8,8,8,512]{4,3,2,1,0:T(8,128)} %shard_map.55) | data formatting | bytes 6291456
where the time goes:
time: 69.9 us; the launch traced here: 69.7 us
  Pallas kernels  65.7 us (94%)
  local copies, waits for them, and re-layouts  4.03 us (6%)
    pallas_call x1, Pallas kernels, on_device(): pl.pallas_call(functools.partial(kernel, n_row, n_col, agg), out_shape=ja...  65.7 us
    unnamed x1, local copies, waits for them, and re-layouts  4.03 us

commit v1 on v0

--- a/solution.py
+++ b/solution.py
@@ -16,8 +16,8 @@
     n_row, n_col, agg,
     load_h, diag_h, coup_h, aggr_h, inv_h, out_h,
     load_v, diag_v, coup, ag, inv, wgt, first, second, resid, third, out_v,
-    xh, yh, ys, agx, agy, agys, agz, gath, tabs,
-    in_sem, send_sem, recv_sem, g_send, g_recv, out_sem,
+    xh, yh, ys, relay, agx, agy, agys, agz, gath, tabs,
+    in_sem, load_sem, send_sem, recv_sem, y_send, y_recv, r_send, r_recv, g_send, g_recv, out_sem,
 ):
     rhs, xs = load_v.shape[1], load_v.shape[2]
     zts = load_v.shape[4] // LANES
@@ -27,16 +27,29 @@
     other = 1 - dep
     own_rows = 3 * agg
 
-    copies = [
-        pltpu.make_async_copy(diag_h, diag_v, in_sem.at[0]),
-        pltpu.make_async_copy(load_h, load_v, in_sem.at[1]),
-        pltpu.make_async_copy(aggr_h, ag, in_sem.at[2]),
-        pltpu.make_async_copy(coup_h, coup, in_sem.at[3]),
-        pltpu.make_async_copy(
-            inv_h.at[0, 0, pl.ds(pl.multiple_of(row * own_rows, SUB), own_rows), :], inv, in_sem.at[4]
-        ),
+    def order(k):
+        return jnp.where(k < xs - 2, k + 1, jnp.where(k == xs - 2, 0, xs - 1))
+
+    def load_copy(x):
+        return pltpu.make_async_copy(load_h.at[:, :, x], load_v.at[:, :, x], load_sem.at[x])
+
+    diagonal = [
+        pltpu.make_async_copy(diag_h.at[c, c], diag_v.at[c, c], in_sem.at[3 * c + c]) for c in range(3)
     ]
-    for copy in copies:
+    off_diagonal = [
+        pltpu.make_async_copy(diag_h.at[a, c], diag_v.at[a, c], in_sem.at[3 * a + c])
+        for a in range(3) for c in range(3) if a != c
+    ]
+    aggr_copy = pltpu.make_async_copy(aggr_h, ag, in_sem.at[9])
+    coup_copy = pltpu.make_async_copy(coup_h, coup, in_sem.at[10])
+    inv_copy = pltpu.make_async_copy(
+        inv_h.at[0, 0, pl.ds(pl.multiple_of(row * own_rows, SUB), own_rows), :], inv, in_sem.at[11]
+    )
+    for copy in diagonal:
+        copy.start()
+    for x in [*range(1, xs - 1), 0, xs - 1]:
+        load_copy(x).start()
+    for copy in (aggr_copy, *off_diagonal, coup_copy, inv_copy):
         copy.start()
 
     sides = [
@@ -52,6 +65,11 @@
         @pl.when(has)
         def _():
             pl.semaphore_signal(barrier, inc=1, device_id=device, device_id_type=MESH)
+    relays = [(col > 1, {"col": col - 2}), (col < n_col - 2, {"col": col + 2})]
+    for has, device in relays:
+        @pl.when(has)
+        def _():
+            pl.semaphore_signal(barrier, inc=1, device_id=device, device_id_type=MESH)
     pl.semaphore_signal(barrier, inc=1, device_id={"dep": other}, device_id_type=MESH)
 
     def zlane(zt):
@@ -72,34 +90,6 @@
 
         lax.fori_loop(0, xs, body_z, 0)
 
-    zero_edges(first)
-    copies[0].wait()
-    copies[1].wait()
-
-    def scale(x, _):
-        for c in range(3):
-            wgt[c, x] = 0.8 / diag_v[c, c, x]
-
-        def inner(zt, _):
-            for c in range(3):
-                value = wgt[c, x, :, zlane(zt)][None] * load_v[c, :, x, :, zlane(zt)]
-                first[x + 1, zt + 1, c * rhs * SUB:(c + 1) * rhs * SUB, :] = value.reshape(rhs * SUB, LANES)
-            return 0
-
-        lax.fori_loop(0, zts, inner, 0)
-        return 0
-
-    lax.fori_loop(0, xs, scale, 0)
-
-    def pack_y(field, slot):
-        def body(i, _):
-            x, zt = i // zts, i % zts
-            for s in range(2):
-                ys[slot, s, x, zt] = field[x + 1, zt + 1, pl.ds(s * (SUB - 1), 3 * rhs, stride=SUB), :]
-            return 0
-
-        lax.fori_loop(0, xs * zts, body, 0)
-
     def remote(src, dst, sem, device):
         return pltpu.make_async_remote_copy(
             src_ref=src, dst_ref=dst, send_sem=send_sem.at[sem], recv_sem=recv_sem.at[sem],
@@ -108,21 +98,20 @@
 
     def to_sides(base, pieces):
         found = []
-        for s, (has, device) in enumerate(sides):
+        for s, (has, device) in enumerate(sides[:len(pieces)]):
             src, dst = pieces[s]
             found.append((has, remote(src, dst, base + (s ^ 1), device)))
         return found
 
     def from_sides(base, pieces):
         found = []
-        for s, (has, device) in enumerate(sides):
+        for s, (has, device) in enumerate(sides[:len(pieces)]):
             src, dst = pieces[s ^ 1]
             found.append((has, remote(src, dst, base + s, device)))
         return found
 
-    def start_all(found, only=range(4)):
-        for s in only:
-            has, copy = found[s]
+    def start_all(found):
+        for has, copy in found:
             pl.when(has)(copy.start)
 
     def wait_sends(found):
@@ -133,9 +122,62 @@
         return [
             (field.at[1, pl.ds(1, zts)], xh.at[slot, 1]),
             (field.at[xs, pl.ds(1, zts)], xh.at[slot, 0]),
-            (ys.at[slot, 0], yh.at[slot, 1]),
-            (ys.at[slot, 1], yh.at[slot, 0]),
         ]
+
+    odd = lax.rem(col, 2)
+    straight = col + 1 - 2 * odd
+    has_across = jnp.where(odd == 1, col < n_col - 1, col > 0)
+    across = col - 1 + 2 * odd
+    corner = col - 2 + 4 * odd
+    passes_on = jnp.where(odd == 1, col > 1, col < n_col - 2)
+    pass_to = col + 1 - 2 * odd
+    half = xs // 2
+
+    def y_copy(src, dst, send, recv, device):
+        return pltpu.make_async_remote_copy(
+            src_ref=src, dst_ref=dst, send_sem=send, recv_sem=recv,
+            device_id={"col": device}, device_id_type=MESH,
+        )
+
+    def straight_copy(slot, k):
+        x = order(k)
+        return y_copy(ys.at[slot, 1 - odd, x], yh.at[slot, odd, x], y_send.at[slot, 0, k],
+                      y_recv.at[slot, odd, x], straight)
+
+    def across_copy(slot, k, part):
+        x = order(k)
+        if part == 0:
+            return y_copy(ys.at[slot, odd, x], relay.at[slot, k // 2], y_send.at[slot, 1, k],
+                          r_recv.at[slot, k // 2], corner)
+        return y_copy(ys.at[slot, odd, x], yh.at[slot, 1 - odd, x], y_send.at[slot, 1, k],
+                      y_recv.at[slot, 1 - odd, x], across)
+
+    def pass_copy(slot, j):
+        x = order(2 * j)
+        return y_copy(relay.at[slot, j], yh.at[slot, 1 - odd, x], r_send.at[slot, j],
+                      y_recv.at[slot, 1 - odd, x], pass_to)
+
+    def pass_on(slot, j):
+        @pl.when(passes_on)
+        def _():
+            across_copy(slot, 2 * j, 0).wait_recv()
+            pass_copy(slot, j).start()
+
+    def send_y(slot, k, part):
+        @pl.when(has_across)
+        def _():
+            across_copy(slot, k, part).start()
+
+        straight_copy(slot, k).start()
+
+    def wait_y(slot, s, x):
+        y_copy(ys.at[slot, s, x], yh.at[slot, s, x], y_send.at[slot, 0, 0], y_recv.at[slot, s, x],
+               straight).wait_recv()
+
+    def pack_y(field, slot, x):
+        for zt in range(zts):
+            for s in range(2):
+                ys[slot, s, x, zt] = field[x + 1, zt + 1, pl.ds(s * (SUB - 1), 3 * rhs, stride=SUB), :]
 
     own_z = (1 - dep) * (zts - 1) + 1
     halo_z = (1 - dep) * (zts + 1)
@@ -144,15 +186,35 @@
     def z_copy(field, sem):
         return remote(field.at[pl.ds(1, xs), own_z], field.at[pl.ds(1, xs), far_z], sem, {"dep": other})
 
-    pack_y(first, 0)
-    pl.semaphore_wait(barrier, n_row - 1 + 1 + (col > 0).astype(jnp.int32) + (col < n_col - 1).astype(jnp.int32))
+    waits = [sides[2][0], sides[3][0], relays[0][0], relays[1][0]]
+    pl.semaphore_wait(barrier, n_row + sum(has.astype(jnp.int32) for has in waits))
+    for copy in diagonal:
+        copy.wait()
+
+    def scale(j, _):
+        for part in range(2):
+            k = 2 * j + part
+            x = order(k)
+            load_copy(x).wait()
+            for c in range(3):
+                weight = 0.8 / diag_v[c, c, x]
+                wgt[c, x] = weight
+                for zt in range(zts):
+                    zl = slice(zt * LANES, (zt + 1) * LANES)
+                    value = weight[:, zl][None] * load_v[c, :, x, :, zl]
+                    first[x + 1, zt + 1, c * rhs * SUB:(c + 1) * rhs * SUB, :] = value.reshape(rhs * SUB, LANES)
+            pack_y(first, 0, x)
+            send_y(0, k, part)
+        return 0
+
+    lax.fori_loop(0, half, scale, 0)
     p1 = face_pieces(first, 0)
     e1 = to_sides(0, p1)
-    start_all(e1, (2, 3, 0, 1))
+    start_all(e1)
     z1 = z_copy(first, 4)
     z1.start()
 
-    copies[2].wait()
+    aggr_copy.wait()
     for x in range(xs):
         for s in range(2):
             y = s * (SUB - 1)
@@ -167,11 +229,13 @@
         ag.at[:, :, zlane((1 - dep) * (zts - 1))], agz, 14, {"dep": other}
     )
     za.start()
+    zero_edges(first)
     zero_edges(second)
     zero_edges(third)
     tabs[...] = jnp.zeros_like(tabs)
     gath[row] = jnp.zeros((3 * rhs, LANES), jnp.float32)
-    copies[3].wait()
+    for copy in (*off_diagonal, coup_copy):
+        copy.wait()
     z1.wait_recv()
 
     lane = lax.broadcasted_iota(jnp.int32, (rb, SUB, LANES), 2)
@@ -212,14 +276,23 @@
                     total[a] = total[a] - coup[d, a, c, x, :, zl][None] * near
         return own, total
 
-    def sweep(body):
+    def sweep(body, slot=None):
         def run(i, _):
             x, zt = i // zts, i % zts
             for r0 in range(0, rhs, rb):
                 body(x, zt, r0)
             return 0
 
-        lax.fori_loop(0, xs * zts, run, 0)
+        if slot is None:
+            lax.fori_loop(0, xs * zts, run, 0)
+            return
+
+        def quarter(j, _):
+            lax.fori_loop(2 * zts * j, 2 * zts * (j + 1), run, 0)
+            pass_on(slot, j)
+            return 0
+
+        lax.fori_loop(0, half, quarter, 0)
 
     def smooth(x, zt, r0):
         own, total = operate(first, x, zt, r0)
@@ -228,7 +301,7 @@
             value = own[a] + wgt[a, x, :, zl][None] * (load_v[a, r0:r0 + rb, x, :, zl] - total[a])
             second[x + 1, zt + 1, tile_rows(a, r0), :] = value.reshape(rb * SUB, LANES)
 
-    sweep(smooth)
+    sweep(smooth, 0)
 
     def fix_x(field, off, s, slot, weighted):
         x = s * (xs - 1)
@@ -252,13 +325,11 @@
 
         lax.fori_loop(0, zts, body, 0)
 
-    def fix_y(field, off, s, slot, weighted):
+    def fix_y(field, off, s, slot, weighted, x):
         y = s * (SUB - 1)
         d = 3 - s
-
-        def body(i, _):
-            x, zt = i // zts, i % zts
-            zl = zlane(zt)
+        for zt in range(zts):
+            zl = slice(zt * LANES, (zt + 1) * LANES)
             near = [yh[slot, s, x, zt, c * rhs:(c + 1) * rhs, :] for c in range(3)]
             for a in range(3):
                 t = coup[d, a, 0, x, y:y + 1, zl] * near[0]
@@ -268,26 +339,38 @@
                     t = wgt[a, x, y:y + 1, zl] * t
                 at = pl.ds(a * rhs * SUB + y, rhs, stride=SUB)
                 field[x + off, zt + off, at, :] = field[x + off, zt + off, at, :] + t
-            return 0
-
-        lax.fori_loop(0, xs * zts, body, 0)
-
-    def fix_arrived(arrivals, field, off, slot, weighted):
+
+    def fix_x_arrived(arrivals, field, off, slot, weighted):
         for s, (has, copy) in enumerate(arrivals):
             @pl.when(has)
             def _():
-                if copy is not None:
-                    copy.wait_recv()
-                if s < 2:
-                    fix_x(field, off, s, slot, weighted)
-                else:
-                    fix_y(field, off, s - 2, slot, weighted)
-
-    fix_arrived(from_sides(0, p1), second, 1, 0, True)
-    pack_y(second, 1)
+                copy.wait_recv()
+                fix_x(field, off, s, slot, weighted)
+
+    def fix_y_arrived(field, off, slot, weighted, x):
+        for s in range(2):
+            @pl.when(sides[2 + s][0])
+            def _():
+                wait_y(slot, s, x)
+                fix_y(field, off, s, slot, weighted, x)
+
+    def renew(j, _):
+        @pl.when(j == half - 1)
+        def _():
+            fix_x_arrived(from_sides(0, p1), second, 1, 0, True)
+
+        for part in range(2):
+            k = 2 * j + part
+            x = order(k)
+            fix_y_arrived(second, 1, 0, True, x)
+            pack_y(second, 1, x)
+            send_y(1, k, part)
+        return 0
+
+    lax.fori_loop(0, half, renew, 0)
     p2 = face_pieces(second, 1)
     e2 = to_sides(5, p2)
-    start_all(e2, (2, 3, 0, 1))
+    start_all(e2)
     z2 = z_copy(second, 9)
     z2.start()
     z2.wait_recv()
@@ -299,14 +382,12 @@
             value = load_v[a, r0:r0 + rb, x, :, zl] - total[a]
             resid[x, zt, tile_rows(a, r0), :] = value.reshape(rb * SUB, LANES)
 
-    sweep(defect)
-    copies[4].wait()
-    fix_arrived(from_sides(5, p2), resid, 0, 1, False)
+    sweep(defect, 1)
 
     number = lax.broadcasted_iota(jnp.int32, (agg, zts * LANES), 0)
 
-    def restrict(x, total):
-        for y in range(SUB):
+    def restrict(x, total, lines):
+        for y in lines:
             value = jnp.concatenate(
                 [resid[x, zt, pl.ds(y, 3 * rhs, stride=SUB), :] for zt in range(zts)], axis=1
             )
@@ -318,7 +399,27 @@
             )
         return total
 
-    sums = lax.fori_loop(0, xs, restrict, jnp.zeros((6 * rhs, agg), jnp.float32))
+    inner = range(1, SUB - 1)
+    sums = lax.fori_loop(
+        1, xs - 1, lambda x, total: restrict(x, total, inner), jnp.zeros((6 * rhs, agg), jnp.float32)
+    )
+
+    def finish(k, total):
+        x = order(k)
+        fix_y_arrived(resid, 0, 1, False, x)
+        return restrict(x, total, (0, SUB - 1))
+
+    sums = lax.fori_loop(0, xs - 2, finish, sums)
+    fix_x_arrived(from_sides(5, p2), resid, 0, 1, False)
+
+    def finish_edge(k, total):
+        x = order(k)
+        total = restrict(x, total, inner)
+        fix_y_arrived(resid, 0, 1, False, x)
+        return restrict(x, total, (0, SUB - 1))
+
+    sums = lax.fori_loop(xs - 2, xs, finish_edge, sums)
+    inv_copy.wait()
     gath[row, :, 0:agg] = sums[:3 * rhs] + sums[3 * rhs:]
     gathers = []
     for step in range(1, n_row):
@@ -402,17 +503,20 @@
                 lax.fori_loop(0, zts, body, 0)
                 fix_x(out_v, 0, s, 2, True)
             else:
-                def body(zt, _):
-                    for x in range(xs):
-                        index = jnp.broadcast_to(agy[s - 2, x:x + 1, zlane(zt)], (SUB, LANES))
+                for x in range(xs):
+                    for zt in range(zts):
+                        zl = slice(zt * LANES, (zt + 1) * LANES)
+                        index = jnp.broadcast_to(agy[s - 2, x:x + 1, zl], (SUB, LANES))
                         for c in range(3):
                             yh[2, s - 2, x, zt, c * rhs:(c + 1) * rhs, :] = look(
                                 tabs[1 + s, c * rhs:(c + 1) * rhs, :], index
                             )
+
+                def body_y(x, _):
+                    fix_y(out_v, 0, s - 2, 2, True, x)
                     return 0
 
-                lax.fori_loop(0, zts, body, 0)
-                fix_y(out_v, 0, s - 2, 2, True)
+                lax.fori_loop(0, xs, body_y, 0)
 
     outs = []
     for x in range(xs):
@@ -428,6 +532,22 @@
         wait_sends(found)
     for copy in (z1, z2, za, zt_copy, *gathers):
         copy.wait_send()
+
+    def wait_y_sends(j, _):
+        for slot in range(2):
+            for part in range(2):
+                straight_copy(slot, 2 * j + part).wait_send()
+
+                @pl.when(has_across)
+                def _():
+                    across_copy(slot, 2 * j + part, part).wait_send()
+
+            @pl.when(passes_on)
+            def _():
+                pass_copy(slot, j).wait_send()
+        return 0
+
+    lax.fori_loop(0, half, wait_y_sends, 0)
     for copy in outs:
         copy.wait()
 
@@ -458,15 +578,21 @@
             pltpu.VMEM((3, 2, zts, rows, LANES), f32),
             pltpu.VMEM((3, 2, xs, zts, 3 * rhs, LANES), f32),
             pltpu.VMEM((2, 2, xs, zts, 3 * rhs, LANES), f32),
+            pltpu.VMEM((2, xs // 2, zts, 3 * rhs, LANES), f32),
             pltpu.VMEM((2, sub, depth), jnp.int32),
             pltpu.VMEM((2, xs, depth), jnp.int32),
             pltpu.VMEM((2, xs, depth), jnp.int32),
             pltpu.VMEM((xs, sub, LANES), jnp.int32),
             pltpu.VMEM((n_row, 3 * rhs, LANES), f32),
             pltpu.VMEM((6, 3 * rhs, LANES), f32),
-            dma((5,)),
+            dma((12,)),
+            dma((xs,)),
             dma((20,)),
             dma((20,)),
+            dma((2, 2, xs)),
+            dma((2, 2, xs)),
+            dma((2, xs // 2)),
+            dma((2, xs // 2)),
             dma((n_row - 1,)),
             dma((n_row - 1,)),
             dma((xs * zts,)),

time: 69.9 us -> 56.4 us (0.81)
  the two profiles are of different devices: /device:TPU:4 before, /device:TPU:0 now
where the time goes in v1:
time: 56.4 us; the launch traced here: 56.2 us
  Pallas kernels  52.2 us (93%)
  local copies, waits for them, and re-layouts  4.03 us (7%)
    pallas_call x1, Pallas kernels, on_device(): pl.pallas_call(functools.partial(kernel, n_row, n_col, agg), out_shape=ja...  52.2 us
    unnamed x1, local copies, waits for them, and re-layouts  4.03 us

profile of v1, /device:TPU:0, one launch (start us, length us, event | category | flops | bytes accessed | tf_op | source)
XLA Modules:
  0.0 56.2 jit_solution(4334778994554584980)
XLA Ops:
  0.0 52.2 %shard_map.55 = f32[3,8,8,8,512]{4,3,2,1,0:T(8,128)} custom-call(f32[3,8,8,8,512]{4,3,2,1,0:T(8,128)} %load_h.1, f32[3,3,8,8,512]{4,3,2,1,0:T(8,128)} %diag_h.1, f32[6,3,3,8,8,512]{5,4,3,2,1,0:T(8,128)} %coup_h.1, s32[8,8,512]{2,1,0:T(8,128)} %aggr_h.1, f32[1,1,768,768]{3,2,1,0:T(8,128)} %inv_h.1), custom_call_target="tpu_custom_call" | custom-call | tf_op jit(solution)/shard_map/pallas_call | solution.py:565
  52.2 4.0 %copy.7 = f32[3,8,8,8,512]{4,3,2,1,0:T(8,128)} copy(f32[3,8,8,8,512]{4,3,2,1,0:T(8,128)} %shard_map.55) | data formatting | bytes 6291456

commit v2 on v1

--- a/solution.py
+++ b/solution.py
@@ -14,10 +14,10 @@
 
 def kernel(
     n_row, n_col, agg,
-    load_h, diag_h, coup_h, aggr_h, inv_h, out_h,
-    load_v, diag_v, coup, ag, inv, wgt, first, second, resid, third, out_v,
+    load_h, diag_h, coup_h, aggr_h, inv_h, out_v,
+    load_v, diag_v, coup, ag, inv, wgt, first, second, resid, third,
     xh, yh, ys, relay, agx, agy, agys, agz, gath, tabs,
-    in_sem, load_sem, send_sem, recv_sem, y_send, y_recv, r_send, r_recv, g_send, g_recv, out_sem,
+    in_sem, load_sem, send_sem, recv_sem, y_send, y_recv, r_send, r_recv, g_send, g_recv,
 ):
     rhs, xs = load_v.shape[1], load_v.shape[2]
     zts = load_v.shape[4] // LANES
@@ -518,16 +518,6 @@
 
                 lax.fori_loop(0, xs, body_y, 0)
 
-    outs = []
-    for x in range(xs):
-        for zt in range(zts):
-            outs.append(pltpu.make_async_copy(
-                out_v.at[x, zt].reshape(3, rhs, SUB, LANES),
-                out_h.at[:, :, x, :, pl.ds(zt * LANES, LANES)],
-                out_sem.at[x * zts + zt],
-            ))
-    for copy in outs:
-        copy.start()
     for found in (e1, e2, ea, et):
         wait_sends(found)
     for copy in (z1, z2, za, zt_copy, *gathers):
@@ -548,7 +538,22 @@
         return 0
 
     lax.fori_loop(0, half, wait_y_sends, 0)
-    for copy in outs:
+
+
+def deliver(tiles, out_h, sem):
+    xs, zts = tiles.shape[0], tiles.shape[1]
+    _, rhs, _, sub, _ = out_h.shape
+    copies = []
+    for x in range(xs):
+        for zt in range(zts):
+            copies.append(pltpu.make_async_copy(
+                tiles.at[x, zt].reshape(3, rhs, sub, LANES),
+                out_h.at[:, :, x, :, pl.ds(zt * LANES, LANES)],
+                sem.at[x * zts + zt],
+            ))
+    for copy in copies:
+        copy.start()
+    for copy in copies:
         copy.wait()
 
 
@@ -562,11 +567,11 @@
     dma = pltpu.SemaphoreType.DMA
     field = pltpu.VMEM((xs + 2, zts + 2, rows, LANES), f32)
     block = pltpu.VMEM((xs, zts, rows, LANES), f32)
-    return pl.pallas_call(
+    tiles = pl.pallas_call(
         functools.partial(kernel, n_row, n_col, agg),
-        out_shape=jax.ShapeDtypeStruct(load.shape, f32),
+        out_shape=pltpu.VMEM((xs, zts, rows, LANES), f32),
         in_specs=[pl.BlockSpec(memory_space=pl.ANY)] * 5,
-        out_specs=pl.BlockSpec(memory_space=pl.ANY),
+        out_specs=pl.BlockSpec(memory_space=pltpu.VMEM),
         scratch_shapes=[
             pltpu.VMEM(load.shape, f32),
             pltpu.VMEM(diagonal_block.shape, f32),
@@ -574,7 +579,7 @@
             pltpu.VMEM(aggregates.shape, jnp.int32),
             pltpu.VMEM((3 * agg, ncg), f32),
             pltpu.VMEM((3, xs, sub, depth), f32),
-            field, field, block, field, block,
+            field, field, block, field,
             pltpu.VMEM((3, 2, zts, rows, LANES), f32),
             pltpu.VMEM((3, 2, xs, zts, 3 * rhs, LANES), f32),
             pltpu.VMEM((2, 2, xs, zts, 3 * rhs, LANES), f32),
@@ -595,12 +600,19 @@
             dma((2, xs // 2)),
             dma((n_row - 1,)),
             dma((n_row - 1,)),
-            dma((xs * zts,)),
         ],
         compiler_params=pltpu.CompilerParams(
-            collective_id=0, has_side_effects=True, vmem_limit_bytes=60 * 2**20
+            collective_id=0, has_side_effects=True, vmem_limit_bytes=52 * 2**20
         ),
     )(load, diagonal_block, coupling, aggregates, coarse_inverse)
+    return pl.pallas_call(
+        deliver,
+        out_shape=jax.ShapeDtypeStruct(load.shape, f32),
+        in_specs=[pl.BlockSpec(memory_space=pl.ANY)],
+        out_specs=pl.BlockSpec(memory_space=pl.ANY),
+        scratch_shapes=[dma((xs * zts,))],
+        compiler_params=pltpu.CompilerParams(vmem_limit_bytes=2**20),
+    )(tiles)
 
 
 def solution(mesh):

time: 56.4 us -> 52.4 us (0.929)
  local copies, waits for them, and re-layouts: 4.03 us -> 0 us
    unnamed x1 -> x0, local copies, waits for them, and re-layouts: 4.03 us -> none
    pallas_call x1 -> x2, Pallas kernels: 52.2 us -> 52.2 us  [the longest x1 50.3 us: on_device(): pl.pallas_call(functools.partial(kernel, n_row, n_col, agg), out_shape=pl...]
where the time goes in v2:
time: 52.4 us; the launch traced here: 52.2 us
  Pallas kernels  52.2 us (100%)
    pallas_call x1, Pallas kernels, on_device(): pl.pallas_call(functools.partial(kernel, n_row, n_col, agg), out_shape=pl...  50.3 us
    pallas_call x1, Pallas kernels, on_device(): pl.pallas_call(deliver, out_shape=jax.ShapeDtypeStruct(load.shape, f32),...  1.92 us

profile of v2, /device:TPU:0, one launch (start us, length us, event | category | flops | bytes accessed | tf_op | source)
XLA Modules:
  0.0 52.2 jit_solution(2515938124439570845)
XLA Ops:
  0.0 50.3 %shard_map.55.tiles = f32[8,4,192,128]{3,2,1,0:T(8,128)S(1)} custom-call(f32[3,8,8,8,512]{4,3,2,1,0:T(8,128)} %load_h.1, f32[3,3,8,8,512]{4,3,2,1,0:T(8,128)} %diag_h.1, f32[6,3,3,8,8,512]{5,4,3,2,1,0:T(8,128)} %coup_h.1, s32[8,8,512]{2,1,0:T(8,128)} %aggr_h.1, f32[1,1,768,768]{3,2,1,0:T(8,128)} %inv_h.1), custom_call_target="tpu_custom_call" | custom-call | tf_op jit(solution)/shard_map/pallas_call | solution.py:570
  50.3 1.9 %shard_map.56 = f32[3,8,8,8,512]{4,3,2,1,0:T(8,128)} custom-call(f32[8,4,192,128]{3,2,1,0:T(8,128)S(1)} %shard_map.55.tiles), custom_call_target="tpu_custom_call" | custom-call | tf_op jit(solution)/shard_map/pallas_call | solution.py:608

commit v3 on v2

--- a/solution.py
+++ b/solution.py
@@ -15,7 +15,7 @@
 def kernel(
     n_row, n_col, agg,
     load_h, diag_h, coup_h, aggr_h, inv_h, out_v,
-    load_v, diag_v, coup, ag, inv, wgt, first, second, resid, third,
+    load_v, diag_v, coup, ag, inv, inv_parts, wgt, first, second, resid, third,
     xh, yh, ys, relay, agx, agy, agys, agz, gath, tabs,
     in_sem, load_sem, send_sem, recv_sem, y_send, y_recv, r_send, r_recv, g_send, g_recv,
 ):
@@ -289,7 +289,10 @@
 
         def quarter(j, _):
             lax.fori_loop(2 * zts * j, 2 * zts * (j + 1), run, 0)
-            pass_on(slot, j)
+            if slot == 0:
+                pass_on(slot, j)
+            else:
+                pl.when(j == 0)(lambda: pass_on(slot, half - 1))
             return 0
 
         lax.fori_loop(0, half, quarter, 0)
@@ -365,6 +368,11 @@
             fix_y_arrived(second, 1, 0, True, x)
             pack_y(second, 1, x)
             send_y(1, k, part)
+
+        @pl.when(j > 0)
+        def _():
+            pass_on(1, j - 1)
+
         return 0
 
     lax.fori_loop(0, half, renew, 0)
@@ -399,6 +407,9 @@
             )
         return total
 
+    inv_copy.wait()
+    inv_parts[0] = inv[...].astype(jnp.bfloat16)
+    inv_parts[1] = (inv[...] - inv_parts[0].astype(jnp.float32)).astype(jnp.bfloat16)
     inner = range(1, SUB - 1)
     sums = lax.fori_loop(
         1, xs - 1, lambda x, total: restrict(x, total, inner), jnp.zeros((6 * rhs, agg), jnp.float32)
@@ -419,7 +430,6 @@
         return restrict(x, total, (0, SUB - 1))
 
     sums = lax.fori_loop(xs - 2, xs, finish_edge, sums)
-    inv_copy.wait()
     gath[row, :, 0:agg] = sums[:3 * rhs] + sums[3 * rhs:]
     gathers = []
     for step in range(1, n_row):
@@ -438,10 +448,13 @@
     vector = jnp.concatenate(
         [gath[i, c * rhs:(c + 1) * rhs, 0:agg] for i in range(n_row) for c in range(3)], axis=1
     )
-    solved = lax.dot_general(
-        vector, inv[...], (((1,), (1,)), ((), ())), precision=lax.Precision.HIGHEST,
-        preferred_element_type=jnp.float32,
+    high = vector.astype(jnp.bfloat16).astype(jnp.float32)
+    both = jnp.concatenate([high, vector - high], axis=0).astype(jnp.bfloat16)
+    products = sum(
+        lax.dot_general(both, inv_parts[i], (((1,), (1,)), ((), ())), preferred_element_type=jnp.float32)
+        for i in (1, 0)
     )
+    solved = products[rhs:] + products[:rhs]
     for c in range(3):
         tabs[0, c * rhs:(c + 1) * rhs, 0:agg] = solved[:, c * agg:(c + 1) * agg]
     pt = [(tabs.at[0], tabs.at[1 + (s ^ 1)]) for s in range(4)]
@@ -482,41 +495,43 @@
             value = tile(second, x + 1, zt + 1, a, r0) + own[a] + wgt[a, x, :, zl][None] * left
             out_v[x, zt, tile_rows(a, r0), :] = value.reshape(rb * SUB, LANES)
 
-    sweep(final)
-
     arrived_t, arrived_a = from_sides(15, pt), from_sides(10, pa)
-    for s in range(4):
-        has = sides[s][0]
-
-        @pl.when(has)
+    for s in range(2):
+        @pl.when(sides[s][0])
         def _():
             arrived_t[s][1].wait_recv()
             arrived_a[s][1].wait_recv()
-            if s < 2:
-                def body(zt, _):
-                    index = agx[s, :, zlane(zt)]
-                    for k in range(3 * rhs):
-                        table = jnp.broadcast_to(tabs[1 + s, k:k + 1, :], (SUB, LANES))
-                        xh[2, s, zt, k * SUB:(k + 1) * SUB, :] = look(table, index)
-                    return 0
-
-                lax.fori_loop(0, zts, body, 0)
-                fix_x(out_v, 0, s, 2, True)
-            else:
-                for x in range(xs):
-                    for zt in range(zts):
-                        zl = slice(zt * LANES, (zt + 1) * LANES)
-                        index = jnp.broadcast_to(agy[s - 2, x:x + 1, zl], (SUB, LANES))
-                        for c in range(3):
-                            yh[2, s - 2, x, zt, c * rhs:(c + 1) * rhs, :] = look(
-                                tabs[1 + s, c * rhs:(c + 1) * rhs, :], index
-                            )
-
-                def body_y(x, _):
-                    fix_y(out_v, 0, s - 2, 2, True, x)
-                    return 0
-
-                lax.fori_loop(0, xs, body_y, 0)
+
+            def body(zt, _):
+                index = agx[s, :, zlane(zt)]
+                for k in range(3 * rhs):
+                    table = jnp.broadcast_to(tabs[1 + s, k:k + 1, :], (SUB, LANES))
+                    third[s * (xs + 1), zt + 1, k * SUB:(k + 1) * SUB, :] = look(table, index)
+                return 0
+
+            lax.fori_loop(0, zts, body, 0)
+
+    sweep(final)
+
+    for s in range(2, 4):
+        @pl.when(sides[s][0])
+        def _():
+            arrived_t[s][1].wait_recv()
+            arrived_a[s][1].wait_recv()
+            for x in range(xs):
+                for zt in range(zts):
+                    zl = slice(zt * LANES, (zt + 1) * LANES)
+                    index = jnp.broadcast_to(agy[s - 2, x:x + 1, zl], (SUB, LANES))
+                    for c in range(3):
+                        yh[2, s - 2, x, zt, c * rhs:(c + 1) * rhs, :] = look(
+                            tabs[1 + s, c * rhs:(c + 1) * rhs, :], index
+                        )
+
+            def body_y(x, _):
+                fix_y(out_v, 0, s - 2, 2, True, x)
+                return 0
+
+            lax.fori_loop(0, xs, body_y, 0)
 
     for found in (e1, e2, ea, et):
         wait_sends(found)
@@ -578,9 +593,10 @@
             pltpu.VMEM(coupling.shape, f32),
             pltpu.VMEM(aggregates.shape, jnp.int32),
             pltpu.VMEM((3 * agg, ncg), f32),
+            pltpu.VMEM((2, 3 * agg, ncg), jnp.bfloat16),
             pltpu.VMEM((3, xs, sub, depth), f32),
             field, field, block, field,
-            pltpu.VMEM((3, 2, zts, rows, LANES), f32),
+            pltpu.VMEM((2, 2, zts, rows, LANES), f32),
             pltpu.VMEM((3, 2, xs, zts, 3 * rhs, LANES), f32),
             pltpu.VMEM((2, 2, xs, zts, 3 * rhs, LANES), f32),
             pltpu.VMEM((2, xs // 2, zts, 3 * rhs, LANES), f32),

time: 52.4 us -> 53.2 us (1.015)
  Pallas kernels: 52.2 us -> 53 us
    pallas_call x1, Pallas kernels: 50.3 us -> 51.1 us  [on_device(): pl.pallas_call(functools.partial(kernel, n_row, n_col, agg), out_shape=pl...]
where the time goes in v3:
time: 53.2 us; the launch traced here: 53 us
  Pallas kernels  53 us (100%)
    pallas_call x1, Pallas kernels, on_device(): pl.pallas_call(functools.partial(kernel, n_row, n_col, agg), out_shape=pl...  51.1 us
    pallas_call x1, Pallas kernels, on_device(): pl.pallas_call(deliver, out_shape=jax.ShapeDtypeStruct(load.shape, f32),...  1.92 us

profile of v3, /device:TPU:0, one launch (start us, length us, event | category | flops | bytes accessed | tf_op | source)
XLA Modules:
  0.0 53.0 jit_solution(10472799342029759472)
XLA Ops:
  0.0 51.1 %shard_map.55.tiles = f32[8,4,192,128]{3,2,1,0:T(8,128)S(1)} custom-call(f32[3,8,8,8,512]{4,3,2,1,0:T(8,128)} %load_h.1, f32[3,3,8,8,512]{4,3,2,1,0:T(8,128)} %diag_h.1, f32[6,3,3,8,8,512]{5,4,3,2,1,0:T(8,128)} %coup_h.1, s32[8,8,512]{2,1,0:T(8,128)} %aggr_h.1, f32[1,1,768,768]{3,2,1,0:T(8,128)} %inv_h.1), custom_call_target="tpu_custom_call" | custom-call | tf_op jit(solution)/shard_map/pallas_call | solution.py:585
  51.1 1.9 %shard_map.56 = f32[3,8,8,8,512]{4,3,2,1,0:T(8,128)} custom-call(f32[8,4,192,128]{3,2,1,0:T(8,128)S(1)} %shard_map.55.tiles), custom_call_target="tpu_custom_call" | custom-call | tf_op jit(solution)/shard_map/pallas_call | solution.py:624
